TPU v7x, 32 devices: a whole 2x2x4 slice. The times are simulated.
32 devices in a mesh: shard: 8 (over y, x, core), rep: 4 (over z).
Axes of the slice: x: 2, y: 2, z: 4, core: 2. Of those that a mesh axis runs over, the one named last changes fastest.
Arguments:
- docs: bfloat16 [4096, 16384], P('shard', 'rep')
- pattern: int32 [32, 128], P('shard', 'rep'), may hold values 0 or 1
- owners: int32 [4], replicated, may hold values from 0 to 7
Outputs:
- scores: bfloat16 [4, 256, 4096], P(None, ('shard', 'rep'))
All inputs are finite; a program needn't handle non-finite values. No bound on the sum of `pattern` on one device may be relied on, other than what follows from the above.
Results may differ from a plain program's by a relative error of at most 0.001.
Values may be sent and summed in bfloat16 or wider, within the bound.
A program may use at most 128 MiB of HBM per device.

v0:
```python
import math

import jax
import jax.numpy as jnp
from jax import lax
from jax.sharding import PartitionSpec as P

TERMS = 16384
QUERY = 256
STEPS = 4


EPSILON = 1e-06
CLIP_LEVEL = 1.5


def from_root(block, axis, owner):
    block = jnp.where(lax.axis_index(axis) == owner, block, jnp.zeros_like(block))
    return lax.psum(block, axis)


def on_device(docs, pattern, owners):
    n_shard = lax.axis_size("shard")
    n_rep = lax.axis_size("rep")
    shard_index = lax.axis_index("shard")
    rep_index = lax.axis_index("rep")
    doc_rows, term_cols = docs.shape
    tile_edge = 128
    row_share = QUERY // (n_shard * n_rep)
    weights = pattern.astype(jnp.bfloat16)
    masked = (
        docs.reshape(doc_rows // tile_edge, tile_edge, term_cols // tile_edge, tile_edge)
        * weights[:, None, :, None]
    ).reshape(doc_rows, term_cols)
    partial_sq = jnp.einsum("dt,dt->d", masked, masked, preferred_element_type=jnp.float32)
    doc_sq = lax.psum(partial_sq, "rep")
    inverse = lax.rsqrt(doc_sq + EPSILON)
    all_inverse = lax.all_gather(inverse, "shard", axis=0, tiled=True)
    sharpen = math.sqrt(TERMS) * 0.5
    results = []
    for step_index in range(STEPS):
        offset = step_index % (doc_rows // QUERY) * QUERY
        candidate = masked[offset : offset + QUERY]
        queries = from_root(candidate, "shard", owners[step_index])
        offset = step_index % (doc_rows // QUERY) * QUERY
        first_global = owners[step_index] * doc_rows + offset
        query_inv = lax.dynamic_slice_in_dim(all_inverse, first_global, QUERY, 0).reshape(
            n_shard, n_rep, row_share
        )
        similar = lax.dot_general(
            queries, masked, (((1,), (1,)), ((), ())), preferred_element_type=jnp.float32
        )
        summed = lax.psum(similar, "rep").reshape(n_shard, n_rep, row_share, doc_rows)
        own_rows = lax.dynamic_index_in_dim(summed, rep_index, 1, keepdims=False)
        received = lax.all_to_all(own_rows, "shard", split_axis=0, concat_axis=2, tiled=True)[0]
        shard_inv = lax.dynamic_index_in_dim(query_inv, shard_index, 0, keepdims=False)
        row_inv = lax.dynamic_index_in_dim(shard_inv, rep_index, 0, keepdims=False)
        scaled = received * row_inv[:, None] * all_inverse[None, :] * sharpen
        results.append(jnp.clip(scaled, -CLIP_LEVEL, CLIP_LEVEL).astype(jnp.bfloat16))
    return jnp.stack(results)


def solution(mesh):
    return jax.shard_map(
        on_device,
        mesh=mesh,
        in_specs=(P("shard", "rep"), P("shard", "rep"), P()),
        out_specs=P(None, ("shard", "rep"), None),
        check_vma=False,
    )
```

profile of v0, /device:TPU:0, one launch (start us, length us, event | category | flops | bytes accessed | tf_op | source)
XLA Modules:
  0.0 303.0 jit_solution(16923501395865591032)
XLA Ops:
  6.5 0.0 all-reduce.7.cloned.1.call-start
  6.5 1.5 fusion.6
  10.5 0.7 convert_element_type.43
  11.2 3.4 %copy.8 = bf16[64,8,32,128]{3,2,1,0:T(8,128)(2,1)S(1)} copy(bf16[64,8,32,128]{3,1,2,0:T(8,128)(2,1)} %bitcast.80) | data formatting | bytes 8388608
  14.6 0.3 bitcast_multiply_fusion.1
  15.0 0.6 broadcast_select_fusion.3
  15.6 6.0 %copy_bitcast_fusion.2 = (bf16[256,4096]{1,0:T(8,128)(2,1)}, bf16[256,4096]{1,0:T(8,128)(2,1)}) fusion(bf16[32,8,32,128]{3,2,1,0:T(8,128)(2,1)S(1)} %bitcast.86, bf16[32,8,32,128]{3,2,1,0:T(8,128)(2,1)S(1)} %bitcast.85), kind=kLoop, calls=%fused_computation.6 | loop fusion | bytes 8388608 | tf_op jit(solution)/shard_map/jit(_where)/select_n | solution.py:18
  21.6 6.0 %copy_bitcast_fusion = (bf16[256,4096]{1,0:T(8,128)(2,1)}, bf16[256,4096]{1,0:T(8,128)(2,1)}) fusion(bf16[32,8,32,128]{3,2,1,0:T(8,128)(2,1)S(1)} %bitcast.84, bf16[32,8,32,128]{3,2,1,0:T(8,128)(2,1)S(1)} %bitcast.83), kind=kLoop, calls=%fused_computation.4 | loop fusion | bytes 8388608 | tf_op jit(solution)/shard_map/jit(_where)/select_n | solution.py:18
  27.6 0.0 all-reduce.7.cloned.1.call-update
  27.7 0.2 all-reduce.5.cloned.1.call-start
  27.9 0.0 copy-start
  27.9 0.6 mul.187
  28.5 1.6 copy-done
  30.1 3.7 %fusion = (f32[512]{0:T(512)S(1)}, bf16[512,4096]{1,0:T(8,128)(2,1)}) fusion(bf16[512,4096]{1,0:T(8,128)(2,1)S(1)} %copy-done, bf16[64,8,32,128]{3,2,1,0:T(8,128)(2,1)S(1)} %bitcast.81), kind=kLoop, calls=%fused_computation.1 | loop fusion | flops 8388096 | bytes 12584960 | tf_op jit(solution)/shard_map/dt,dt->d/dot_general | solution.py:35
  33.8 124.2 %all-reduce.7.cloned.1.call-done = (bf16[256,4096]{1,0:T(8,128)(2,1)}, bf16[256,4096]{1,0:T(8,128)(2,1)}, bf16[256,4096]{1,0:T(8,128)(2,1)}, bf16[256,4096]{1,0:T(8,128)(2,1)}) async-done(((bf16[256,4096]{1,0:T(8,128)(2,1)}, bf16[256,4096]{1,0:T(8,128)(2,1)}, bf16[256,4096]{1,0:T(8,128)(2,1)}, bf16[256,4096]{1,0:T(8,128)(2,1)}), (bf16[256,4096]{1,0:T(8,128)(2,1)}, bf16[256,4096]{1,0:T(8,128)(2,1)}, ...) | async-done | bytes 8388624 | tf_op jit(solution)/shard_map/psum | solution.py:19
  158.0 0.0 copy-start.1
  158.0 0.0 copy-start.4
  158.0 5.1 %fusion.7 = f32[256,512]{1,0:T(8,128)} fusion(bf16[256,4096]{1,0:T(8,128)(2,1)} %get-tuple-element.12, bf16[512,4096]{1,0:T(8,128)(2,1)} %get-tuple-element.14), kind=kOutput, calls=%fused_computation.32 | convolution fusion | flops 1073741824 | bytes 6815744 | tf_op jit(solution)/shard_map/dot_general | solution.py:50
  163.1 0.0 copy-done.1
  163.1 0.0 copy-done.4
  163.2 0.0 copy-start.3
  163.2 2.1 fusion.8
  165.3 0.0 copy-done.3
  165.3 0.0 copy-start.2
  165.3 2.1 fusion.9
  167.3 0.0 copy-done.2
  167.3 2.1 fusion.10
  169.4 0.0 all-reduce.5.cloned.1.call-update
  172.0 12.0 %psum.65 = f32[512]{0:T(512)S(1)} all-reduce(f32[512]{0:T(512)S(1)} %get-tuple-element.13), channel_id=1, replica_groups=mesh['shard'=8,'rep'=4] {'rep'}, use_global_device_ids=true, to_apply=%region_2.3 | all-reduce | flops 512 | bytes 4096 | tf_op jit(solution)/shard_map/psum | solution.py:36
  184.0 8.8 %all-gather = f32[8,1,512]{2,1,0:T(1,128)S(1)} all-gather(f32[1,1,512]{2,1,0:T(1,128)S(1)} %bitcast.97), channel_id=1, replica_groups=mesh['shard'=8,'rep'=4] {'shard'}, dimensions={0}, use_global_device_ids=true | all-gather | bytes 18432 | tf_op jit(solution)/shard_map/all_gather | solution.py:38
  192.8 0.1 fusion.5
  192.9 0.1 reshape.348
  193.0 0.1 reshape.350
  193.1 64.9 %all-reduce.5.cloned.1.call-done = (f32[8,4,8,512]{3,2,1,0:T(8,128)}, f32[8,4,8,512]{3,2,1,0:T(8,128)}, f32[8,4,8,512]{3,2,1,0:T(8,128)}, f32[8,4,8,512]{3,2,1,0:T(8,128)}) async-done(((f32[8,4,8,512]{3,2,1,0:T(8,128)}, f32[8,4,8,512]{3,2,1,0:T(8,128)}, f32[8,4,8,512]{3,2,1,0:T(8,128)}, f32[8,4,8,512]{3,2,1,0:T(8,128)}), (f32[8,4,8,512]{3,2,1,0:T(8,128)}, f32[8,4,8,512]{3,2,1,0:T(8,128)}, ...) | async-done | bytes 2097168 | tf_op jit(solution)/shard_map/psum | solution.py:53
  258.0 1.6 dynamic-slice_bitcast_fusion.2
  259.6 3.7 %all-to-all-start.1 = ((f32[8,8,512]{2,1,0:T(8,128)}), f32[8,8,512]{2,1,0:T(8,128)S(1)}, u32[]{:S(2)}, u32[]{:S(2)}) async-start(f32[8,8,512]{2,1,0:T(8,128)} %dynamic-slice_bitcast_fusion.2), calls=%async_computation.1 | async-start | bytes 262144 | tf_op jit(solution)/shard_map/all_to_all | solution.py:55
  263.2 1.6 dynamic-slice_bitcast_fusion.1
  264.8 4.0 %all-to-all-done.1 = f32[8,8,512]{2,1,0:T(8,128)S(1)} async-done(((f32[8,8,512]{2,1,0:T(8,128)}), f32[8,8,512]{2,1,0:T(8,128)S(1)}, u32[]{:S(2)}, u32[]{:S(2)}) %all-to-all-start.1) | async-done | bytes 131104 | tf_op jit(solution)/shard_map/all_to_all | solution.py:55
  268.8 3.4 %all-to-all-start.2 = ((f32[8,8,512]{2,1,0:T(8,128)}), f32[8,8,512]{2,1,0:T(8,128)S(1)}, u32[]{:S(2)}, u32[]{:S(2)}) async-start(f32[8,8,512]{2,1,0:T(8,128)} %dynamic-slice_bitcast_fusion.1), calls=%async_computation.2 | async-start | bytes 262144 | tf_op jit(solution)/shard_map/all_to_all | solution.py:55
  272.2 1.6 dynamic-slice_bitcast_fusion
  273.7 3.9 %all-to-all-done.2 = f32[8,8,512]{2,1,0:T(8,128)S(1)} async-done(((f32[8,8,512]{2,1,0:T(8,128)}), f32[8,8,512]{2,1,0:T(8,128)S(1)}, u32[]{:S(2)}, u32[]{:S(2)}) %all-to-all-start.2) | async-done | bytes 131104 | tf_op jit(solution)/shard_map/all_to_all | solution.py:55
  277.6 3.4 %all-to-all-start.3 = ((f32[8,8,512]{2,1,0:T(8,128)}), f32[8,8,512]{2,1,0:T(8,128)S(1)}, u32[]{:S(2)}, u32[]{:S(2)}) async-start(f32[8,8,512]{2,1,0:T(8,128)} %dynamic-slice_bitcast_fusion), calls=%async_computation.3 | async-start | bytes 262144 | tf_op jit(solution)/shard_map/all_to_all | solution.py:55
  281.0 1.6 dynamic-slice_bitcast_fusion.3
  282.6 3.9 %all-to-all-done.3 = f32[8,8,512]{2,1,0:T(8,128)S(1)} async-done(((f32[8,8,512]{2,1,0:T(8,128)}), f32[8,8,512]{2,1,0:T(8,128)S(1)}, u32[]{:S(2)}, u32[]{:S(2)}) %all-to-all-start.3) | async-done | bytes 131104 | tf_op jit(solution)/shard_map/all_to_all | solution.py:55
  286.5 3.4 %all-to-all-start = ((f32[8,8,512]{2,1,0:T(8,128)}), f32[8,8,512]{2,1,0:T(8,128)S(1)}, u32[]{:S(2)}, u32[]{:S(2)}) async-start(f32[8,8,512]{2,1,0:T(8,128)} %dynamic-slice_bitcast_fusion.3), calls=%async_computation | async-start | bytes 262144 | tf_op jit(solution)/shard_map/all_to_all | solution.py:55
  289.9 0.1 reshape.352
  290.0 0.1 reshape.354
  290.1 5.2 %all-to-all-done = f32[8,8,512]{2,1,0:T(8,128)S(1)} async-done(((f32[8,8,512]{2,1,0:T(8,128)}), f32[8,8,512]{2,1,0:T(8,128)S(1)}, u32[]{:S(2)}, u32[]{:S(2)}) %all-to-all-start) | async-done | bytes 131104 | tf_op jit(solution)/shard_map/all_to_all | solution.py:55
  295.3 0.1 clamp_convert_fusion.3
  295.5 0.7 pad_maximum_fusion
  (3 shorter events, 0.0 us)
Async XLA Ops:
  6.5 151.5 %all-reduce.7.cloned.1.call-start = ((), (), s32[]{:S(2)}) async-start(), calls=%async_computation.5 | async-start | bytes 16777216 | tf_op jit(solution)/shard_map/psum | solution.py:19
  27.7 230.4 %all-reduce.5.cloned.1.call-start = ((), (), s32[]{:S(2)}) async-start(), calls=%async_computation.4 | async-start | bytes 4194304 | tf_op jit(solution)/shard_map/psum | solution.py:53
  27.9 2.2 copy-start
  158.0 5.1 %copy-start.1 = (bf16[512,4096]{1,0:T(8,128)(2,1)S(1)}, bf16[512,4096]{1,0:T(8,128)(2,1)}, u32[]{:S(2)}) copy-start(bf16[512,4096]{1,0:T(8,128)(2,1)} %get-tuple-element.14) | copy-start | bytes 12582916
  158.0 5.1 %copy-start.4 = (bf16[256,4096]{1,0:T(8,128)(2,1)S(1)}, bf16[256,4096]{1,0:T(8,128)(2,1)}, u32[]{:S(2)}) copy-start(bf16[256,4096]{1,0:T(8,128)(2,1)} %get-tuple-element.11) | copy-start | bytes 6291460
  163.2 2.1 copy-start.3
  165.3 2.1 copy-start.2
  259.6 9.2 %all-to-all-start.1 = ((f32[8,8,512]{2,1,0:T(8,128)}), f32[8,8,512]{2,1,0:T(8,128)S(1)}, u32[]{:S(2)}, u32[]{:S(2)}) async-start(f32[8,8,512]{2,1,0:T(8,128)} %dynamic-slice_bitcast_fusion.2), calls=%async_computation.1 | async-start | bytes 262144 | tf_op jit(solution)/shard_map/all_to_all | solution.py:55
  268.8 8.8 %all-to-all-start.2 = ((f32[8,8,512]{2,1,0:T(8,128)}), f32[8,8,512]{2,1,0:T(8,128)S(1)}, u32[]{:S(2)}, u32[]{:S(2)}) async-start(f32[8,8,512]{2,1,0:T(8,128)} %dynamic-slice_bitcast_fusion.1), calls=%async_computation.2 | async-start | bytes 262144 | tf_op jit(solution)/shard_map/all_to_all | solution.py:55
  277.6 8.8 %all-to-all-start.3 = ((f32[8,8,512]{2,1,0:T(8,128)}), f32[8,8,512]{2,1,0:T(8,128)S(1)}, u32[]{:S(2)}, u32[]{:S(2)}) async-start(f32[8,8,512]{2,1,0:T(8,128)} %dynamic-slice_bitcast_fusion), calls=%async_computation.3 | async-start | bytes 262144 | tf_op jit(solution)/shard_map/all_to_all | solution.py:55
  286.5 8.8 %all-to-all-start = ((f32[8,8,512]{2,1,0:T(8,128)}), f32[8,8,512]{2,1,0:T(8,128)S(1)}, u32[]{:S(2)}, u32[]{:S(2)}) async-start(f32[8,8,512]{2,1,0:T(8,128)} %dynamic-slice_bitcast_fusion.3), calls=%async_computation | async-start | bytes 262144 | tf_op jit(solution)/shard_map/all_to_all | solution.py:55
Sparse Core Ops, SparseCore 0:
  27.8 130.2 all-reduce.6
  169.6 88.4 all-reduce.4
where the time goes:
time: 304 us; the launch traced here: 303 us
  waiting for transfers between devices  206 us (68%)
  local copies, waits for them, and re-layouts  25.9 us (9%)
  blocking collectives  20.9 us (7%)
  between operations  18.6 us (6%)
  starting transfers between devices  14 us (5%)
  matrix products  11.4 us (4%)
  other arithmetic  6.24 us (2%)
    psum x1, waiting for transfers between devices, from_root(): return lax.psum(block, axis)  124 us
    psum x1, waiting for transfers between devices, on_device(): lax.psum(similar, 'rep').reshape(n_shard, n_rep, row_share, doc_rows)  64.9 us
    all_to_all x4, waiting for transfers between devices, on_device(): lax.all_to_all(own_rows, 'shard', split_axis=0, concat_axis=2, tiled=True)  17 us
    all_to_all x4, starting transfers between devices, on_device(): lax.all_to_all(own_rows, 'shard', split_axis=0, concat_axis=2, tiled=True)  13.8 us
    select_n x2, local copies, waits for them, and re-layouts, from_root(): jnp.where(lax.axis_index(axis) == owner, block, jnp.zeros_like(block))  12.1 us
    psum x1, blocking collectives, on_device(): doc_sq = lax.psum(partial_sq, 'rep')  12 us
    dot_general x4, matrix products, on_device(): lax.dot_general(queries, masked, (((1,), (1,)), ((), ())), preferred_elem...  11.4 us
    all_gather x1, blocking collectives, on_device(): all_inverse = lax.all_gather(inverse, 'shard', axis=0, tiled=True)  8.82 us
  transfers between devices with their start and end apart: 6, of which 6 were waited for; matrix products, arithmetic and copies ran while one was open for 3% of the time, Pallas kernels for 0%

commit v1 on v0

--- a/solution.py
+++ b/solution.py
@@ -3,15 +3,309 @@
 import jax
 import jax.numpy as jnp
 from jax import lax
+from jax.experimental import pallas as pl
+from jax.experimental.pallas import tpu as pltpu
 from jax.sharding import PartitionSpec as P
 
 TERMS = 16384
 QUERY = 256
 STEPS = 4
+EDGE = 128
 
 
 EPSILON = 1e-06
 CLIP_LEVEL = 1.5
+SHARPEN = math.sqrt(TERMS) * 0.5
+
+CHIPS = 4
+REPS = 4
+CHUNK = 256
+GROUPS = ((0, 1), (2, 3))
+MESH = pl.DeviceIdType.MESH
+
+
+def ring(index):
+    return index + (index // 2) * (1 - 2 * (index % 2))
+
+
+def joined(
+    owners, pattern, docs, out,
+    mine, cross, stage, arrived, partial, sibling, summed, others, norm_parts, inverse, query_column, held, final, landed,
+    cross_send, cross_recv, ring_send, ring_recv, core_send, core_recv, rep_send, rep_recv,
+    norm_send, norm_recv, inv_send, inv_recv, out_send, out_recv,
+):
+    shard = lax.axis_index("shard")
+    rep = lax.axis_index("rep")
+    core = shard % 2
+    chip = shard // 2
+    place = ring(chip)
+    mate = chip * 2 + 1 - core
+    onward = ring((place + 1 + 2 * core) % CHIPS) * 2 + core
+    chunks = mine.shape[0]
+    rows = docs.shape[0]
+    shards = 2 * CHIPS
+
+    barrier = pltpu.get_barrier_semaphore()
+    for d in range(1, shards):
+        pl.semaphore_signal(barrier, inc=1, device_id=((shard + d) % shards, rep), device_id_type=MESH)
+    for d in range(1, REPS):
+        pl.semaphore_signal(barrier, inc=1, device_id=(shard, (rep + d) % REPS), device_id_type=MESH)
+    pl.semaphore_wait(barrier, shards - 1 + REPS - 1)
+
+    def copy(src, dst, send, recv, to):
+        return pltpu.make_async_remote_copy(
+            src_ref=src, dst_ref=dst, send_sem=send, recv_sem=recv, device_id=to, device_id_type=MESH
+        )
+
+    def cross_copy(k):
+        return copy(cross.at[k], mine.at[k, core], cross_send.at[k], cross_recv.at[k], (mate, rep))
+
+    def masked_chunk(half, k):
+        index = half * chunks + k
+        parts = []
+        for i in range(rows // EDGE):
+            cols = []
+            for j in range(CHUNK // EDGE):
+                weight = pattern[i, index * (CHUNK // EDGE) + j].astype(jnp.float32)
+                block = docs[i * EDGE : (i + 1) * EDGE, pl.ds(pl.multiple_of(index * CHUNK + j * EDGE, EDGE), EDGE)]
+                cols.append(block * jnp.full((EDGE, EDGE), weight, jnp.float32).astype(jnp.bfloat16))
+            parts.append(cols)
+        return parts
+
+    def put(ref, k, lead, parts, squares):
+        added = []
+        for i, cols in enumerate(parts):
+            total = None
+            for j, block in enumerate(cols):
+                at = (slice(i * EDGE, (i + 1) * EDGE), slice(j * EDGE, (j + 1) * EDGE))
+                ref[(k, *lead, *at)] = block
+                wide = block.astype(jnp.float32)
+                total = wide * wide if total is None else total + wide * wide
+            added.append(total)
+        return squares + jnp.concatenate(added, axis=0)
+
+    def to_mate(k, squares):
+        squares = put(cross, k, (), masked_chunk(1 - core, k), squares)
+        cross_copy(k).start()
+        return squares
+
+    def to_self(k, squares):
+        return put(mine, k, (core,), masked_chunk(core, k), squares)
+
+    squares = lax.fori_loop(0, chunks, to_mate, jnp.zeros((rows, EDGE), jnp.float32))
+    squares = lax.fori_loop(0, chunks, to_self, squares)
+
+    def as_row(column):
+        return jnp.transpose(jnp.broadcast_to(column, (column.shape[0], 128)))[:8]
+
+    norm_parts[0] = as_row(jnp.sum(squares, axis=1, keepdims=True))
+
+    def norm_copy(d):
+        return copy(norm_parts.at[0], norm_parts.at[d], norm_send.at[d], norm_recv.at[d], (shard, (rep + d) % REPS))
+
+    for d in range(1, REPS):
+        norm_copy(d).start()
+
+    for k in range(chunks):
+        cross_copy(k).wait_recv()
+
+    def inv_copy(d):
+        return copy(
+            inverse.at[shard], inverse.at[shard], inv_send.at[d], inv_recv.at[d], ((shard + d) % shards, rep)
+        )
+
+    def inv_arrival(d):
+        slot = inverse.at[(shard + shards - d) % shards]
+        return copy(slot, slot, inv_send.at[d], inv_recv.at[d], ((shard + d) % shards, rep))
+
+    def norms():
+        for d in range(1, REPS):
+            norm_copy(d).wait_recv()
+        inverse[shard] = lax.rsqrt(norm_parts[0] + norm_parts[1] + norm_parts[2] + norm_parts[3] + EPSILON)
+        for d in range(1, shards):
+            inv_copy(d).start()
+
+    def ring_copy(s, t):
+        return copy(stage.at[s, t], arrived.at[s, t], ring_send.at[s, t], ring_recv.at[s, t], (onward, rep))
+
+    def core_copy(s):
+        return copy(partial.at[s, :, 1 - core], sibling.at[s], core_send.at[s], core_recv.at[s], (mate, rep))
+
+    def rep_copy(s, d):
+        to = (rep + d) % REPS
+        return copy(summed.at[s, :, to], others.at[s, d - 1], rep_send.at[s, d - 1], rep_recv.at[s, d - 1], (shard, to))
+
+    def out_copy(g, d):
+        to = (chip + d) % CHIPS
+        lines = pl.ds(g * 16, 16)
+        return copy(
+            final.at[to, lines], landed.at[chip, lines], out_send.at[g, d - 1], out_recv.at[g, d - 1],
+            (to * 2 + core, rep),
+        )
+
+    def out_arrival(g, d):
+        lines = pl.ds(g * 16, 16)
+        slot = landed.at[(chip + CHIPS - d) % CHIPS, lines]
+        return copy(slot, slot, out_send.at[g, d - 1], out_recv.at[g, d - 1], (((chip + d) % CHIPS) * 2 + core, rep))
+
+    def to_sibling(g):
+        for s in GROUPS[g]:
+            core_copy(s).start()
+
+    def to_reps(g):
+        for s in GROUPS[g]:
+            core_copy(s).wait_recv()
+            summed[s] = partial[s, :, core] + sibling[s]
+            for d in (2, 1, 3):
+                rep_copy(s, d).start()
+
+    def finish(g):
+        columns = jnp.concatenate([inverse[2 * chip, 0:1, :], inverse[2 * chip + 1, 0:1, :]], axis=1)
+        for s in GROUPS[g]:
+            offset = s % (rows // QUERY) * QUERY
+            line = inverse[owners[s], 0:1, offset : offset + QUERY]
+            query_column[...] = jnp.transpose(jnp.broadcast_to(line, (128, QUERY)))
+            for d in range(1, REPS):
+                rep_copy(s, d).wait_recv()
+            for to in range(CHIPS):
+                first = pl.multiple_of((to * 2 + core) * 32 + rep * 8, 8)
+                total = summed[s, to, rep] + others[s, 0, to] + others[s, 1, to] + others[s, 2, to]
+                query_inv = query_column[pl.ds(first, 8), 0:1]
+                scaled = total * query_inv * columns * SHARPEN
+                held[s % 2, to] = jnp.clip(scaled, -CLIP_LEVEL, CLIP_LEVEL)
+        for to in range(CHIPS):
+            final[to, g * 16 : (g + 1) * 16, :] = jnp.concatenate([held[0, to], held[1, to]], axis=0).astype(jnp.bfloat16)
+        for d in range(1, CHIPS):
+            out_copy(g, d).start()
+
+    for g, steps in enumerate(GROUPS):
+        for s in steps:
+            partial[s] = jnp.zeros(partial.shape[1:], jnp.float32)
+
+        def body(t, carry, g=g, steps=steps):
+            here = jnp.minimum(t, chunks - 1)
+            for s in steps:
+                half = s % (rows // QUERY) * QUERY
+                first = mine[here, 0, half : half + QUERY, :]
+                second = mine[here, 1, half : half + QUERY, :]
+                own = jnp.where(owners[s] % 2 == 0, first, second)
+                own = jnp.where(t < chunks, own, jnp.zeros_like(own))
+                is_own = owners[s] // 2 == chip
+
+                @pl.when(t == 0)
+                def _():
+                    stage[s, t] = jnp.where(is_own, own, jnp.zeros_like(own))
+
+                @pl.when(t > 0)
+                def _():
+                    ring_copy(s, t - 1).wait_recv()
+                    stage[s, t] = jnp.where(is_own, own, arrived[s, t - 1])
+
+                @pl.when(t < chunks + 2)
+                def _():
+                    ring_copy(s, t).start()
+
+            if g == 0:
+                @pl.when(t == 1)
+                def _():
+                    norms()
+            else:
+                @pl.when(t == 2)
+                def _():
+                    to_reps(g - 1)
+
+                @pl.when(t == chunks + 1)
+                def _():
+                    finish(g - 1)
+
+            for s in steps:
+                away = place + CHIPS - ring(owners[s] // 2)
+                away = jnp.where(core == 0, away, 2 * CHIPS - away) % CHIPS
+                index = jnp.clip(t - away, 0, chunks - 1)
+                block = mine[index].reshape(2 * rows, CHUNK)
+                product = lax.dot_general(
+                    stage[s, t], block, (((1,), (1,)), ((), ())), preferred_element_type=jnp.float32
+                )
+                partial[s] += product.reshape(partial.shape[1:])
+            return carry
+
+        lax.fori_loop(0, chunks + 3, body, 0)
+        if g == 0:
+            for d in range(1, shards):
+                inv_arrival(d).wait_recv()
+        to_sibling(g)
+
+    last = len(GROUPS) - 1
+    to_reps(last)
+    finish(last)
+    for g in range(len(GROUPS)):
+        landed[chip, g * 16 : (g + 1) * 16, :] = final[chip, g * 16 : (g + 1) * 16, :]
+    for g in range(len(GROUPS)):
+        for d in range(1, CHIPS):
+            out_arrival(g, d).wait_recv()
+    for c in range(CHIPS):
+        out[:, c * 2 * rows : (c + 1) * 2 * rows] = landed[c]
+
+    for k in range(chunks):
+        cross_copy(k).wait_send()
+    for d in range(1, REPS):
+        norm_copy(d).wait_send()
+    for d in range(1, shards):
+        inv_copy(d).wait_send()
+    for s in range(STEPS):
+        lax.fori_loop(0, chunks + 2, lambda t, c, s=s: (ring_copy(s, t).wait_send(), c)[1], 0)
+        core_copy(s).wait_send()
+        for d in range(1, REPS):
+            rep_copy(s, d).wait_send()
+    for g in range(len(GROUPS)):
+        for d in range(1, CHIPS):
+            out_copy(g, d).wait_send()
+
+
+def on_ring(docs, pattern, owners):
+    rows, terms = docs.shape
+    chunks = terms // 2 // CHUNK
+    bf16, f32 = jnp.bfloat16, jnp.float32
+    dma = pltpu.SemaphoreType.DMA
+    slots = chunks + 2
+    lines = STEPS * 8
+    buffers = [
+        pltpu.VMEM((chunks, 2, rows, CHUNK), bf16),
+        pltpu.VMEM((chunks, rows, CHUNK), bf16),
+        pltpu.VMEM((STEPS, slots + 1, QUERY, CHUNK), bf16),
+        pltpu.VMEM((STEPS, slots, QUERY, CHUNK), bf16),
+        pltpu.VMEM((STEPS, CHIPS, 2, REPS, 8, 2 * rows), f32),
+        pltpu.VMEM((STEPS, CHIPS, REPS, 8, 2 * rows), f32),
+        pltpu.VMEM((STEPS, CHIPS, REPS, 8, 2 * rows), f32),
+        pltpu.VMEM((STEPS, REPS - 1, CHIPS, 8, 2 * rows), f32),
+        pltpu.VMEM((REPS, 8, rows), f32),
+        pltpu.VMEM((2 * CHIPS, 8, rows), f32),
+        pltpu.VMEM((QUERY, 128), f32),
+        pltpu.VMEM((2, CHIPS, 8, 2 * rows), f32),
+        pltpu.VMEM((CHIPS, lines, 2 * rows), bf16),
+        pltpu.VMEM((CHIPS, lines, 2 * rows), bf16),
+    ]
+    semaphores = []
+    for shape in (
+        (chunks,), (STEPS, slots), (STEPS,), (STEPS, REPS - 1), (REPS,), (2 * CHIPS,), (len(GROUPS), CHIPS - 1)
+    ):
+        semaphores += [dma(shape), dma(shape)]
+    flops = 2 * STEPS * QUERY * rows * terms
+    return pl.pallas_call(
+        joined,
+        out_shape=jax.ShapeDtypeStruct((lines, 2 * CHIPS * rows), bf16),
+        in_specs=[
+            pl.BlockSpec(memory_space=pltpu.SMEM),
+            pl.BlockSpec(memory_space=pltpu.SMEM),
+            pl.BlockSpec(memory_space=pltpu.VMEM),
+        ],
+        out_specs=pl.BlockSpec(memory_space=pltpu.VMEM),
+        scratch_shapes=buffers + semaphores,
+        cost_estimate=pl.CostEstimate(flops=flops, bytes_accessed=rows * terms * 2, transcendentals=0),
+        compiler_params=pltpu.CompilerParams(
+            collective_id=0, has_side_effects=True, vmem_limit_bytes=56 * 2**20
+        ),
+    )(owners, pattern, docs).reshape(STEPS, 8, 2 * CHIPS * rows)
 
 
 def from_root(block, axis, owner):
@@ -61,8 +355,9 @@
 
 
 def solution(mesh):
+    fits = mesh.shape["shard"] == 2 * CHIPS and mesh.shape["rep"] == REPS
     return jax.shard_map(
-        on_device,
+        on_ring if fits else on_device,
         mesh=mesh,
         in_specs=(P("shard", "rep"), P("shard", "rep"), P()),
         out_specs=P(None, ("shard", "rep"), None),

time: 304 us -> 126 us (0.41)
  waiting for transfers between devices: 206 us -> 0 us
  Pallas kernels: 0 us -> 124 us
  local copies, waits for them, and re-layouts: 25.9 us -> 1.67 us
  blocking collectives: 20.9 us -> 0 us
  between operations: 18.6 us -> 0.01 us
  starting transfers between devices: 14 us -> 0 us
  matrix products: 11.4 us -> 0 us
  other arithmetic: 6.24 us -> 0 us
    psum x2 -> x0, waiting for transfers between devices: 189 us -> none  [the longest x1 124 us: from_root(): return lax.psum(block, axis)]
    pallas_call x0 -> x1, Pallas kernels: none -> 124 us  [on_ring(): pl.pallas_call(joined, out_shape=jax.ShapeDtypeStruct((lines, 2 * CHIPS *...]
    all_to_all x4 -> x0, waiting for transfers between devices: 17 us -> none  [on_device(): lax.all_to_all(own_rows, 'shard', split_axis=0, concat_axis=2, tiled=True)]
    all_to_all x4 -> x0, starting transfers between devices: 13.8 us -> none  [on_device(): lax.all_to_all(own_rows, 'shard', split_axis=0, concat_axis=2, tiled=True)]
    select_n x2 -> x0, local copies, waits for them, and re-layouts: 12.1 us -> none  [from_root(): jnp.where(lax.axis_index(axis) == owner, block, jnp.zeros_like(block))]
    psum x1 -> x0, blocking collectives: 12 us -> none  [on_device(): doc_sq = lax.psum(partial_sq, 'rep')]
    dot_general x4 -> x0, matrix products: 11.4 us -> none  [on_device(): lax.dot_general(queries, masked, (((1,), (1,)), ((), ())), preferred_elem...]
    all_gather x1 -> x0, blocking collectives: 8.82 us -> none  [on_device(): all_inverse = lax.all_gather(inverse, 'shard', axis=0, tiled=True)]
  transfers between devices with their start and end apart: 6 -> 0, of which waited for: 6 -> 0; matrix products, arithmetic and copies ran while one was open for 3% -> 0% of each run, Pallas kernels for 0% -> 0%
where the time goes in v1:
time: 126 us
  Pallas kernels  124 us (98%)
  local copies, waits for them, and re-layouts  1.67 us (1%)
    pallas_call x1, Pallas kernels, on_ring(): pl.pallas_call(joined, out_shape=jax.ShapeDtypeStruct((lines, 2 * CHIPS *...  124 us

profile of v1, /device:TPU:0, one launch (start us, length us, event | category | flops | bytes accessed | tf_op | source)
XLA Modules:
  0.0 125.8 jit_solution(4056226608825466058)
XLA Ops:
  0.0 124.2 %shard_map.37 = bf16[32,4096]{1,0:T(8,128)(2,1)} custom-call(s32[4]{0:T(128)} %owners.1, s32[4,32]{1,0:T(4,128)} %pattern.1, bf16[512,4096]{1,0:T(8,128)(2,1)} %docs.1), custom_call_target="tpu_custom_call" | custom-call | flops 4294967296 | bytes 4194304 | tf_op jit(solution)/shard_map/pallas_call | solution.py:294
  124.2 1.7 %copy.5 = bf16[4,8,4096]{2,1,0:T(8,128)(2,1)} copy(bf16[4,8,4096]{2,1,0:T(8,128)(2,1)} %bitcast.1) | data formatting | bytes 524288

commit v2 on v1

--- a/solution.py
+++ b/solution.py
@@ -21,6 +21,9 @@
 REPS = 4
 CHUNK = 256
 GROUPS = ((0, 1), (2, 3))
+STARTS = (0, 3, 6, 9)
+LAG = 2
+PIECES = 4
 MESH = pl.DeviceIdType.MESH
 
 
@@ -30,7 +33,7 @@
 
 def joined(
     owners, pattern, docs, out,
-    mine, cross, stage, arrived, partial, sibling, summed, others, norm_parts, inverse, query_column, held, final, landed,
+    mine, cross, stage, arrived, partial, sibling, summed, near, merged, far, norm_parts, inverse, query_column, held, final, landed,
     cross_send, cross_recv, ring_send, ring_recv, core_send, core_recv, rep_send, rep_recv,
     norm_send, norm_recv, inv_send, inv_recv, out_send, out_recv,
 ):
@@ -106,9 +109,6 @@
     for d in range(1, REPS):
         norm_copy(d).start()
 
-    for k in range(chunks):
-        cross_copy(k).wait_recv()
-
     def inv_copy(d):
         return copy(
             inverse.at[shard], inverse.at[shard], inv_send.at[d], inv_recv.at[d], ((shard + d) % shards, rep)
@@ -125,15 +125,24 @@
         for d in range(1, shards):
             inv_copy(d).start()
 
-    def ring_copy(s, t):
-        return copy(stage.at[s, t], arrived.at[s, t], ring_send.at[s, t], ring_recv.at[s, t], (onward, rep))
+    def ring_copy(s, t, p):
+        lines = pl.ds(p * (QUERY // PIECES), QUERY // PIECES)
+        return copy(
+            stage.at[s, t, lines], arrived.at[s, t, lines], ring_send.at[s, t, p], ring_recv.at[s, t, p], (onward, rep)
+        )
 
     def core_copy(s):
         return copy(partial.at[s, :, 1 - core], sibling.at[s], core_send.at[s], core_recv.at[s], (mate, rep))
 
-    def rep_copy(s, d):
-        to = (rep + d) % REPS
-        return copy(summed.at[s, :, to], others.at[s, d - 1], rep_send.at[s, d - 1], rep_recv.at[s, d - 1], (shard, to))
+    high, low = rep // 2, rep % 2
+
+    def near_copy(s):
+        to = high * 2 + 1 - low
+        return copy(summed.at[s, :, :, 1 - low], near.at[s], rep_send.at[s, 0], rep_recv.at[s, 0], (shard, to))
+
+    def far_copy(s):
+        to = (1 - high) * 2 + low
+        return copy(merged.at[s, :, 1 - high], far.at[s], rep_send.at[s, 1], rep_recv.at[s, 1], (shard, to))
 
     def out_copy(g, d):
         to = (chip + d) % CHIPS
@@ -148,16 +157,15 @@
         slot = landed.at[(chip + CHIPS - d) % CHIPS, lines]
         return copy(slot, slot, out_send.at[g, d - 1], out_recv.at[g, d - 1], (((chip + d) % CHIPS) * 2 + core, rep))
 
-    def to_sibling(g):
-        for s in GROUPS[g]:
-            core_copy(s).start()
-
-    def to_reps(g):
-        for s in GROUPS[g]:
-            core_copy(s).wait_recv()
-            summed[s] = partial[s, :, core] + sibling[s]
-            for d in (2, 1, 3):
-                rep_copy(s, d).start()
+    def to_near(s):
+        core_copy(s).wait_recv()
+        summed[s] = partial[s, :, core] + sibling[s]
+        near_copy(s).start()
+
+    def to_far(s):
+        near_copy(s).wait_recv()
+        merged[s] = summed[s, :, :, low] + near[s]
+        far_copy(s).start()
 
     def finish(g):
         columns = jnp.concatenate([inverse[2 * chip, 0:1, :], inverse[2 * chip + 1, 0:1, :]], axis=1)
@@ -165,11 +173,10 @@
             offset = s % (rows // QUERY) * QUERY
             line = inverse[owners[s], 0:1, offset : offset + QUERY]
             query_column[...] = jnp.transpose(jnp.broadcast_to(line, (128, QUERY)))
-            for d in range(1, REPS):
-                rep_copy(s, d).wait_recv()
+            far_copy(s).wait_recv()
             for to in range(CHIPS):
                 first = pl.multiple_of((to * 2 + core) * 32 + rep * 8, 8)
-                total = summed[s, to, rep] + others[s, 0, to] + others[s, 1, to] + others[s, 2, to]
+                total = merged[s, to, high] + far[s, to]
                 query_inv = query_column[pl.ds(first, 8), 0:1]
                 scaled = total * query_inv * columns * SHARPEN
                 held[s % 2, to] = jnp.clip(scaled, -CLIP_LEVEL, CLIP_LEVEL)
@@ -178,66 +185,106 @@
         for d in range(1, CHIPS):
             out_copy(g, d).start()
 
-    for g, steps in enumerate(GROUPS):
-        for s in steps:
-            partial[s] = jnp.zeros(partial.shape[1:], jnp.float32)
-
-        def body(t, carry, g=g, steps=steps):
-            here = jnp.minimum(t, chunks - 1)
-            for s in steps:
-                half = s % (rows // QUERY) * QUERY
-                first = mine[here, 0, half : half + QUERY, :]
-                second = mine[here, 1, half : half + QUERY, :]
-                own = jnp.where(owners[s] % 2 == 0, first, second)
-                own = jnp.where(t < chunks, own, jnp.zeros_like(own))
-                is_own = owners[s] // 2 == chip
-
-                @pl.when(t == 0)
-                def _():
-                    stage[s, t] = jnp.where(is_own, own, jnp.zeros_like(own))
-
-                @pl.when(t > 0)
-                def _():
-                    ring_copy(s, t - 1).wait_recv()
-                    stage[s, t] = jnp.where(is_own, own, arrived[s, t - 1])
-
-                @pl.when(t < chunks + 2)
-                def _():
-                    ring_copy(s, t).start()
-
-            if g == 0:
-                @pl.when(t == 1)
-                def _():
-                    norms()
-            else:
-                @pl.when(t == 2)
-                def _():
-                    to_reps(g - 1)
-
-                @pl.when(t == chunks + 1)
-                def _():
-                    finish(g - 1)
-
-            for s in steps:
-                away = place + CHIPS - ring(owners[s] // 2)
-                away = jnp.where(core == 0, away, 2 * CHIPS - away) % CHIPS
-                index = jnp.clip(t - away, 0, chunks - 1)
-                block = mine[index].reshape(2 * rows, CHUNK)
-                product = lax.dot_general(
-                    stage[s, t], block, (((1,), (1,)), ((), ())), preferred_element_type=jnp.float32
-                )
-                partial[s] += product.reshape(partial.shape[1:])
-            return carry
-
-        lax.fori_loop(0, chunks + 3, body, 0)
-        if g == 0:
+    for s in range(STEPS):
+        partial[s] = jnp.zeros(partial.shape[1:], jnp.float32)
+
+    def forward(s, t, p):
+        here = jnp.clip(t, 0, chunks - 1)
+        lines = slice(p * (QUERY // PIECES), (p + 1) * (QUERY // PIECES))
+        first = s % (rows // QUERY) * QUERY + lines.start
+        both = [mine[here, c, first : first + QUERY // PIECES, :] for c in range(2)]
+        own = jnp.where(owners[s] % 2 == 0, both[0], both[1])
+        own = jnp.where(t < chunks, own, jnp.zeros_like(own))
+        is_own = owners[s] // 2 == chip
+
+        @pl.when(t == 0)
+        def _():
+            stage[s, t, lines] = jnp.where(is_own, own, jnp.zeros_like(own))
+
+        @pl.when(t > 0)
+        def _():
+            ring_copy(s, t - 1, p).wait_recv()
+            stage[s, t, lines] = jnp.where(is_own, own, arrived[s, t - 1, lines])
+
+        @pl.when(t < chunks + 2)
+        def _():
+            ring_copy(s, t, p).start()
+
+    def multiply(s, t):
+        away = place + CHIPS - ring(owners[s] // 2)
+        away = jnp.where(core == 0, away, 2 * CHIPS - away) % CHIPS
+        index = jnp.clip(t - away, 0, chunks - 1)
+        block = mine[index].reshape(2 * rows, CHUNK)
+        product = lax.dot_general(
+            stage[s, t], block, (((1,), (1,)), ((), ())), preferred_element_type=jnp.float32
+        )
+        partial[s] += product.reshape(partial.shape[1:])
+
+    ends = [start + chunks + 3 for start in STARTS]
+    sums = [end + 1 for end in ends]
+    halves = [end + 3 for end in ends]
+    scored = [max(halves[s] for s in steps) + LAG for steps in GROUPS]
+    slots = max(ends)
+
+    for k in range(chunks):
+        cross_copy(k).wait_recv()
+
+    def slot(now, carry):
+        for p in range(PIECES):
+            for s in range(STEPS):
+                @pl.when((now >= STARTS[s]) & (now < ends[s]))
+                def _(s=s, p=p):
+                    forward(s, now - STARTS[s], p)
+
+        @pl.when(now == 2)
+        def _():
+            norms()
+
+        for s in range(STEPS):
+            if sums[s] < slots:
+                @pl.when(now == sums[s])
+                def _(s=s):
+                    to_near(s)
+
+            if halves[s] < slots:
+                @pl.when(now == halves[s])
+                def _(s=s):
+                    to_far(s)
+
+        @pl.when(now == 6)
+        def _():
             for d in range(1, shards):
                 inv_arrival(d).wait_recv()
-        to_sibling(g)
-
-    last = len(GROUPS) - 1
-    to_reps(last)
-    finish(last)
+
+        for g in range(len(GROUPS)):
+            if scored[g] < slots:
+                @pl.when(now == scored[g])
+                def _(g=g):
+                    finish(g)
+
+        for s in range(STEPS):
+            t = now - STARTS[s]
+
+            @pl.when((t >= 0) & (now < ends[s]))
+            def _(s=s, t=t):
+                multiply(s, t)
+
+            @pl.when(now == ends[s] - 1)
+            def _(s=s):
+                core_copy(s).start()
+
+        return carry
+
+    lax.fori_loop(0, slots, slot, 0)
+    for s in range(STEPS):
+        if sums[s] >= slots:
+            to_near(s)
+    for s in range(STEPS):
+        if halves[s] >= slots:
+            to_far(s)
+    for g in range(len(GROUPS)):
+        if scored[g] >= slots:
+            finish(g)
     for g in range(len(GROUPS)):
         landed[chip, g * 16 : (g + 1) * 16, :] = final[chip, g * 16 : (g + 1) * 16, :]
     for g in range(len(GROUPS)):
@@ -253,10 +300,11 @@
     for d in range(1, shards):
         inv_copy(d).wait_send()
     for s in range(STEPS):
-        lax.fori_loop(0, chunks + 2, lambda t, c, s=s: (ring_copy(s, t).wait_send(), c)[1], 0)
+        for p in range(PIECES):
+            lax.fori_loop(0, chunks + 2, lambda t, c, s=s, p=p: (ring_copy(s, t, p).wait_send(), c)[1], 0)
         core_copy(s).wait_send()
-        for d in range(1, REPS):
-            rep_copy(s, d).wait_send()
+        near_copy(s).wait_send()
+        far_copy(s).wait_send()
     for g in range(len(GROUPS)):
         for d in range(1, CHIPS):
             out_copy(g, d).wait_send()
@@ -274,10 +322,12 @@
         pltpu.VMEM((chunks, rows, CHUNK), bf16),
         pltpu.VMEM((STEPS, slots + 1, QUERY, CHUNK), bf16),
         pltpu.VMEM((STEPS, slots, QUERY, CHUNK), bf16),
-        pltpu.VMEM((STEPS, CHIPS, 2, REPS, 8, 2 * rows), f32),
-        pltpu.VMEM((STEPS, CHIPS, REPS, 8, 2 * rows), f32),
-        pltpu.VMEM((STEPS, CHIPS, REPS, 8, 2 * rows), f32),
-        pltpu.VMEM((STEPS, REPS - 1, CHIPS, 8, 2 * rows), f32),
+        pltpu.VMEM((STEPS, CHIPS, 2, 2, 2, 8, 2 * rows), f32),
+        pltpu.VMEM((STEPS, CHIPS, 2, 2, 8, 2 * rows), f32),
+        pltpu.VMEM((STEPS, CHIPS, 2, 2, 8, 2 * rows), f32),
+        pltpu.VMEM((STEPS, CHIPS, 2, 8, 2 * rows), f32),
+        pltpu.VMEM((STEPS, CHIPS, 2, 8, 2 * rows), f32),
+        pltpu.VMEM((STEPS, CHIPS, 8, 2 * rows), f32),
         pltpu.VMEM((REPS, 8, rows), f32),
         pltpu.VMEM((2 * CHIPS, 8, rows), f32),
         pltpu.VMEM((QUERY, 128), f32),
@@ -287,7 +337,7 @@
     ]
     semaphores = []
     for shape in (
-        (chunks,), (STEPS, slots), (STEPS,), (STEPS, REPS - 1), (REPS,), (2 * CHIPS,), (len(GROUPS), CHIPS - 1)
+        (chunks,), (STEPS, slots, PIECES), (STEPS,), (STEPS, 2), (REPS,), (2 * CHIPS,), (len(GROUPS), CHIPS - 1)
     ):
         semaphores += [dma(shape), dma(shape)]
     flops = 2 * STEPS * QUERY * rows * terms

time: 126 us -> 111 us (0.88)
  Pallas kernels: 124 us -> 109 us
    pallas_call x1, Pallas kernels: 124 us -> 109 us  [on_ring(): pl.pallas_call(joined, out_shape=jax.ShapeDtypeStruct((lines, 2 * CHIPS *...]
where the time goes in v2:
time: 111 us; the launch traced here: 110 us
  Pallas kernels  109 us (98%)
  local copies, waits for them, and re-layouts  1.67 us (2%)
    pallas_call x1, Pallas kernels, on_ring(): pl.pallas_call(joined, out_shape=jax.ShapeDtypeStruct((lines, 2 * CHIPS *...  109 us

profile of v2, /device:TPU:0, one launch (start us, length us, event | category | flops | bytes accessed | tf_op | source)
XLA Modules:
  0.0 110.4 jit_solution(9430896798873984792)
XLA Ops:
  0.0 108.7 %shard_map.37 = bf16[32,4096]{1,0:T(8,128)(2,1)} custom-call(s32[4]{0:T(128)} %owners.1, s32[4,32]{1,0:T(4,128)} %pattern.1, bf16[512,4096]{1,0:T(8,128)(2,1)} %docs.1), custom_call_target="tpu_custom_call" | custom-call | flops 4294967296 | bytes 4194304 | tf_op jit(solution)/shard_map/pallas_call | solution.py:344
  108.7 1.7 %copy.5 = bf16[4,8,4096]{2,1,0:T(8,128)(2,1)} copy(bf16[4,8,4096]{2,1,0:T(8,128)(2,1)} %bitcast.1) | data formatting | bytes 524288
